TPU v7x, 128 devices: a whole 4x4x4 slice. The times are simulated.
128 devices in a mesh: grp: 4 (over x), seq: 16 (over z, y), head: 2 (over core).
Axes of the slice: x: 4, y: 4, z: 4, core: 2. Of those that a mesh axis runs over, the one named last changes fastest.
Arguments:
- enc_ids: int32 [32, 1024], P('grp', 'seq'), may hold values from 0 to 32127
- lengths: int32 [32], P('grp'), may hold values from 1 to 924, as said below
- dec_ids: int32 [32, 128], P('grp', 'seq'), may hold values from 0 to 32127
- target_ids: int32 [32, 128], P('grp', 'seq'), may hold values from 0 to 32127
- loss_mask: int32 [32, 128], P('grp'), may hold values from 0 to 1, as said below
- embedding: bfloat16 [32128, 768], P('head')
- prompt: float32 [100, 768], replicated, may hold values from -6 to 6
- first_moment: float32 [100, 768], replicated, may hold values from -5.722046e-06 to 5.722046e-06
- second_moment: float32 [100, 768], replicated, may hold values from 1.3020833e-13 to 5.208333e-13
- gains: float32 [7, 768], replicated, may hold values from 0.5 to 1.5
- enc_qkv: bfloat16 [768, 2304], replicated, may hold values from -0.21875 to 0.21875
- enc_wo: bfloat16 [768, 768], replicated, may hold values from -0.875 to 0.875
- enc_w1: bfloat16 [768, 3072], replicated, may hold values from -0.21875 to 0.21875
- enc_w2: bfloat16 [3072, 768], replicated, may hold values from -0.109375 to 0.109375
- dec_qkv: bfloat16 [768, 3, 768], P(None, None, 'head'), may hold values from -0.21875 to 0.21875
- dec_wo: bfloat16 [768, 768], P('head'), may hold values from -0.625 to 0.625
- cross_q: bfloat16 [768, 768], P(None, 'head'), may hold values from -0.21875 to 0.21875
- cross_kv: bfloat16 [768, 2, 768], P(None, None, 'head'), may hold values from -0.21875 to 0.21875
- cross_wo: bfloat16 [768, 768], P('head'), may hold values from -0.875 to 0.875
- dec_w1: bfloat16 [768, 3072], P(None, 'head'), may hold values from -0.21875 to 0.21875
- dec_w2: bfloat16 [3072, 768], P('head'), may hold values from -0.109375 to 0.109375
Outputs:
- loss: float32 [], replicated
- grad_norm: float32 [], replicated
- trust_norms: float32 [2], replicated
- first_new: float32 [100, 768], replicated
- second_new: float32 [100, 768], replicated
- prompt_new: float32 [100, 768], replicated
Inputs may be any that keep to these rules, and one draw needn't show every extreme that they name: `lengths`: in each group of 8 consecutive examples one has exactly 924 input tokens. `loss_mask`: the first target of every example counts.
All inputs are finite; a program needn't handle non-finite values.
Results may differ from a plain program's by a relative error of at most 0.00355.
Values may be sent and summed in bfloat16 or wider, within the bound.
A program may use at most 256 MiB of HBM per device.

v0:
```python
import functools

import jax
import jax.numpy as jnp
from jax import lax
from jax.experimental import pallas as pl
from jax.experimental.pallas import tpu as pltpu
from jax.sharding import Mesh
from jax.sharding import PartitionSpec as P

HD = 64
PROMPT = 100
STEP = 5
QUARTERS = 4
SEQ = ("ex", "chip")
CLUSTER = ("chip", "head")
EVERYONE = ("grp", "ex", "chip", "head")
NEG = -1000000000.0

norm_eps = 1e-06
beta_first = 0.5
beta_second = 0.5
adam_eps = 1e-12
decay_rate = 0.01
learn_rate = 0.3
clip_bound = 0.0001


MESH = pl.DeviceIdType.MESH
BF = jnp.bfloat16
F32 = jnp.float32
LEAD_PAD = 32
CHUNK = 1024
RING = 4
LANES = 128


def dot_nn(left, right):
    return lax.dot_general(left, right, (((1,), (0,)), ((), ())), preferred_element_type=F32)


def dot_nt(left, right):
    return lax.dot_general(left, right, (((1,), (1,)), ((), ())), preferred_element_type=F32)


def dot_tn(left, right):
    return lax.dot_general(left, right, (((0,), (0,)), ((), ())), preferred_element_type=F32)


def rms(value, gain):
    return value * lax.rsqrt(jnp.mean(value * value, axis=-1, keepdims=True) + norm_eps) * gain


def rms_grad(value, gain, grad):
    scale = lax.rsqrt(jnp.mean(value * value, axis=-1, keepdims=True) + norm_eps)
    scaled = grad * gain
    inner = jnp.mean(scaled * value, axis=-1, keepdims=True)
    return scale * scaled - value * (scale * scale * scale * inner)


GELU_A = 0.7978845608028654
GELU_B = 0.044715


def gelu(value):
    return 0.5 * value * (1.0 + jnp.tanh(GELU_A * (value + GELU_B * (value * value * value))))


def gelu_grad(value, grad):
    square = value * value
    bend = jnp.tanh(GELU_A * (value + GELU_B * (square * value)))
    slope = 0.5 * (1.0 + bend) + 0.5 * value * (1.0 - bend * bend) * (GELU_A * (1.0 + 3.0 * GELU_B * square))
    return grad * slope


def tiles(count, size, body):
    for index in range(count):
        body(pl.ds(index * size, size))


def each(count, unroll, body):
    def step(index, carry):
        body(index)
        return carry

    if unroll == count:
        for index in range(count):
            body(index)
    else:
        lax.fori_loop(0, count, step, 0, unroll=unroll)


def lanes_at(index, size, base=0):
    if isinstance(index, int):
        return pl.ds(base + index * size, size)
    return pl.ds(pl.multiple_of(base + index * size, LANES), size)


UNROLL = {"attend": 1, "self": 1, "cross": 1, "cross_back": 1, "lead": 1, "vocab": 2}


def main_kernel(
    lengths, picked, prompt, loss_mask, gains,
    enc_qkv, enc_wo, enc_w1, enc_w2, dec_qkv, dec_wo, cross_q, cross_kv, cross_wo, dec_w1, dec_w2, embedding,
    out,
    w_qkv, w_o, w_1, w_2, w_dqkv, w_do, w_cq, w_ckv, w_co, w_d1, w_d2, ring,
    lead, enc_my, enc_in, dec_my, dec_in,
    x0, h1, h2, go, spare, n1, q_s, kv, o_f, o_b, s_f, p_b, lse_e, fade_e, scale_e, stat_e, nb, u, act,
    eo, ckv, dckv, gp_s, gp_r, gown, d_o, dkv, dkv_r, gj, dl,
    y0, a1, m_b, sqkv, so, dx_s, dx_r, cq, cp, cp_b, st_p, st_r, co_r, co, co_b,
    lg, px_s, px_r, a2, a3, du, dact, f_b, tgt, acc, acc_b, acc_r, vl_s, vl_r, gffn, gco, st_g,
    blk, s1_r, s2_r, all_r,
    load_sem, ring_sem, send_sem, recv_sem,
):
    width = x0.shape[1]
    rows = x0.shape[0]
    half = f_b.shape[0]
    own = co.shape[1]
    pairs_e, pairs_d = width // LANES, own // LANES
    head, chip = lax.axis_index("head"), lax.axis_index("chip")
    mate, across = 1 - head, 1 - chip
    me, slot_mate = 2 * chip + head, 2 * chip + mate
    slot_across, slot_diag = 2 * across + head, 2 * across + mate
    to_mate, to_across = {"head": mate}, {"chip": across}
    to_diag = {"chip": across, "head": mate}

    grp, ex = lax.axis_index("grp"), lax.axis_index("ex")
    n_grp, n_ex = lax.axis_size("grp"), lax.axis_size("ex")

    def ex_peer(step):
        return {"ex": lax.rem(ex + step, n_ex)}

    def plane_peer(step):
        place = lax.rem(grp * QUARTERS + me + step, n_grp * QUARTERS)
        member = lax.div(place, QUARTERS)
        side = lax.div(place - member * QUARTERS, 2)
        return {"grp": member, "chip": side, "head": place - member * QUARTERS - 2 * side}

    barrier = pltpu.get_barrier_semaphore()
    friends = [plane_peer(step) for step in range(1, n_grp * QUARTERS)] + [ex_peer(step) for step in range(1, n_ex)]
    for peer in friends:
        pl.semaphore_signal(barrier, inc=1, device_id=peer, device_id_type=MESH)

    def load(index, source, target):
        copy = pltpu.make_async_copy(source, target, load_sem.at[index])
        copy.start()
        return copy

    my_rows = pl.ds(pl.multiple_of(head * rows, rows), rows)
    mate_rows = pl.ds(pl.multiple_of(mate * rows, rows), rows)
    dec_rows = pl.ds(2 * rows, dec_my.shape[0])
    load_x = load(0, picked.at[my_rows], enc_my)
    load_y = load(1, picked.at[dec_rows], dec_my)
    load_qkv = load(2, enc_qkv, w_qkv)
    load_dqkv = load(3, dec_qkv, w_dqkv)
    load_do = load(4, dec_wo, w_do)
    load_cq = load(5, cross_q, w_cq)
    load_o = load(6, enc_wo, w_o)
    load_1 = load(7, enc_w1, w_1)
    load_2 = load(8, enc_w2, w_2)
    load_ckv = load(9, cross_kv, w_ckv)
    load_co = load(10, cross_wo, w_co)
    load_d1 = load(11, dec_w1, w_d1)
    load_d2 = load(12, dec_w2, w_d2)
    leads = PROMPT // QUARTERS

    vocab = embedding.shape[0]
    full = vocab // CHUNK
    tail = vocab - full * CHUNK

    def chunk_copy(index, slot):
        at = pl.ds(pl.multiple_of(index * CHUNK, CHUNK), CHUNK)
        return pltpu.make_async_copy(embedding.at[at], ring.at[slot], ring_sem.at[slot])

    def tail_copy():
        slot = full % RING
        return pltpu.make_async_copy(
            embedding.at[pl.ds(full * CHUNK, tail)], ring.at[slot, pl.ds(0, tail)], ring_sem.at[slot]
        )

    for index in range(RING):
        chunk_copy(index, index).start()

    pl.semaphore_wait(barrier, len(friends))
    sends = []
    block_sem = 17 + 3 * (width // (2 * LANES))

    def send(index, source, target, peer):
        copy = pltpu.make_async_remote_copy(
            src_ref=source,
            dst_ref=target,
            send_sem=send_sem.at[index],
            recv_sem=recv_sem.at[index],
            device_id=peer,
            device_id_type=MESH,
        )
        copy.start()
        sends.append(copy)
        return copy

    blocks = rows // 64
    got_x = []
    for block in range(blocks):
        source = picked.at[pl.ds(pl.multiple_of(mate * rows + block * 64, 64), 64)]
        got_x.append(send(block_sem + block, source, enc_in.at[pl.ds(block * 64, 64)], to_mate))
    got_y = send(1, picked.at[dec_rows], dec_in, to_mate)

    lane = lax.broadcasted_iota(jnp.int32, (1, LANES), 1)
    low_lane = lane < HD
    low_b = jnp.where(low_lane, 1.0, 0.0).astype(BF)
    high_b = jnp.where(low_lane, 0.0, 1.0).astype(BF)
    sides = (low_b, high_b)
    gain = [gains[k : k + 1, :] for k in range(7)]
    gain[6] = gain[6] * width ** (-0.5)
    length = lengths[ex]
    tokens = kv.shape[1] - leads

    def allowed(slots, span, first):
        at = lax.broadcasted_iota(jnp.int32, (1, slots * span), 1)
        slot = at // span
        inner = at - slot * span
        return (inner < leads) | (tokens * (slot + first) + inner - leads < length)

    ok = allowed(4, rows, 0)
    okc = allowed(2, rows, 2 * chip)
    okf = allowed(2, rows, 2 * across)
    okl = allowed(4, LEAD_PAD, 0)
    mask_row = loss_mask[pl.ds(ex, 1), :].astype(F32)
    lane_at = lax.broadcasted_iota(jnp.int32, (half, mask_row.shape[1]), 1)
    row_of = lax.broadcasted_iota(jnp.int32, (half, mask_row.shape[1]), 0)
    own_mask = jnp.where(lane_at == row_of + chip * half, jnp.broadcast_to(mask_row, lane_at.shape), 0.0)
    share = jnp.sum(own_mask, axis=-1, keepdims=True) / jnp.sum(mask_row, axis=-1, keepdims=True)

    load_x.wait()
    got_n, got_m = [], []
    for block in range(blocks):
        part = pl.ds(block * 64, 64)
        got_x[block].wait_recv()
        value = enc_my[part].astype(F32) + enc_in[part].astype(F32)
        if block == 0:
            spot = lax.broadcasted_iota(jnp.int32, (64, width), 0)
            for slot in range(QUARTERS):
                lead[0:leads] = jnp.where(me == slot, prompt[slot * leads : (slot + 1) * leads], lead[0:leads])
            value = jnp.where(spot < leads, lead[...], value)
        x0[part] = value
        n1[me, part] = rms(value, gain[0]).astype(BF)
        mine_n = n1.at[me, part]
        got_n.append(send(block_sem + blocks + block, mine_n, mine_n, to_across))
        got_m.append(send(block_sem + 2 * blocks + block, mine_n, mine_n, to_mate))

    load_qkv.wait()

    def query(at):
        q_s[:, at] = (dot_nn(n1[me], w_qkv[:, at]).astype(BF) * HD ** (-0.5)).astype(BF)

    tiles(width // 256, 256, query)

    load_y.wait()
    got_y.wait_recv()
    all_tgt = y0.shape[0]
    value = dec_my[0:all_tgt].astype(F32) + dec_in[0:all_tgt].astype(F32)
    y0[...] = value
    m_b[...] = rms(value, gain[3]).astype(BF)
    tgt[...] = dec_my[all_tgt : all_tgt + half].astype(F32) + dec_in[all_tgt : all_tgt + half].astype(F32)
    load_dqkv.wait()

    for part in range(3):
        sqkv[:, part * own : (part + 1) * own] = dot_nn(m_b[...], w_dqkv[part]).astype(BF)
    row_at = lax.broadcasted_iota(jnp.int32, (all_tgt, all_tgt), 0)
    col_at = lax.broadcasted_iota(jnp.int32, (all_tgt, all_tgt), 1)
    def self_pair(pair):
        q2 = sqkv[:, lanes_at(pair, LANES)]
        k2 = sqkv[:, lanes_at(pair, LANES, own)]
        v2 = sqkv[:, lanes_at(pair, LANES, 2 * own)]
        outs = []
        for side in sides:
            scores = dot_nt(q2 * side, k2) * HD ** (-0.5)
            scores = jnp.where(col_at <= row_at, scores, NEG)
            top = jnp.max(scores, axis=-1, keepdims=True)
            probs = jnp.exp(scores - top)
            total = jnp.sum(probs, axis=-1, keepdims=True)
            outs.append(dot_nn(probs.astype(BF), v2) / total)
        so[:, lanes_at(pair, LANES)] = jnp.where(low_lane, outs[0], outs[1]).astype(BF)

    each(pairs_d, UNROLL["self"], self_pair)
    load_do.wait()

    def self_out(at):
        dx_s[:, at] = dot_nn(so[...], w_do[:, at]).astype(BF)

    tiles(width // 256, 256, self_out)

    got_d = send(4, dx_s, dx_r, to_mate)
    def forward(block):
        part = n1.at[slot_across, pl.ds(block * 64, 64)]
        return pltpu.make_async_remote_copy(
            src_ref=part,
            dst_ref=part,
            send_sem=send_sem.at[block_sem + 3 * blocks + block],
            recv_sem=recv_sem.at[block_sem + 3 * blocks + block],
            device_id=to_mate,
            device_id_type=MESH,
        )

    def key_value(turn):
        slot = jnp.where(turn < 2, 2 * chip, 2 * across) + jnp.where(turn % 2 == 0, head, mate)

        @pl.when(turn == 1)
        def _():
            for copy in got_m:
                copy.wait_recv()

        @pl.when(turn == 2)
        def _():
            for block in range(blocks):
                got_n[block].wait_recv()
                forward(block).start()

        @pl.when(turn == 3)
        def _():
            for block in range(blocks):
                forward(block).wait_recv()

        for index in range(2 * width // 256):
            at = pl.ds(index * 256, 256)
            kv[slot, :, at] = dot_nn(n1[slot], w_qkv[:, pl.ds(width + index * 256, 256)]).astype(BF)

    def between():
        got_d.wait_recv()
        value = y0[...] + (dx_s[...].astype(F32) + dx_r[...].astype(F32))
        a1[...] = value
        m_b[...] = rms(value, gain[4]).astype(BF)
        load_cq.wait()
        cq[...] = (dot_nn(m_b[...], w_cq[...]).astype(BF) * HD ** (-0.5)).astype(BF)

    def key_values(first, last):
        def body(turn, carry):
            key_value(turn)
            return carry

        lax.fori_loop(first, last, body, 0)

    between()

    keys = 4 * rows

    def scores_of(pair, side, index, slots, allowed_keys):
        k2 = kv[slots, :, lanes_at(pair, LANES)].reshape(2 * rows, LANES)
        v2 = kv[slots, :, lanes_at(pair, LANES, width)].reshape(2 * rows, LANES)
        s_f[index] = dot_nt(q_s[:, lanes_at(pair, LANES)] * side, k2)
        return v2

    def near_pair(pair):
        slots = pl.ds(2 * chip, 2)
        outs = []
        for index, side in enumerate(sides):
            v2 = scores_of(pair, side, index, slots, okc)
            for block in range(rows // 32):
                part = pl.ds(block * 32, 32)
                scores = jnp.where(okc, s_f[index, part], NEG)
                top = jnp.max(scores, axis=-1, keepdims=True)
                probs = jnp.exp(scores - top)
                p_b[index, part] = probs.astype(BF)
                total = jnp.sum(probs, axis=-1, keepdims=True)
                u[part, lanes_at(index * pairs_e + pair, LANES)] = jnp.broadcast_to(total, (32, LANES))
                u[part, lanes_at(index * pairs_e + pair, LANES, 2 * width)] = jnp.broadcast_to(top, (32, LANES))
            outs.append(dot_nn(p_b[index], v2))
        o_f[:, lanes_at(pair, LANES)] = jnp.where(low_lane, outs[0], outs[1])

    def far_pair(pair):
        slots = pl.ds(2 * across, 2)
        outs = []
        for index, side in enumerate(sides):
            v2 = scores_of(pair, side, index, slots, okf)
            for block in range(rows // 32):
                part = pl.ds(block * 32, 32)
                scores = jnp.where(okf, s_f[index, part], NEG)
                near_top = u[part, lanes_at(index * pairs_e + pair, LANES, 2 * width)]
                own_top = jnp.max(scores, axis=-1, keepdims=True)
                top = jnp.maximum(jnp.broadcast_to(own_top, (32, LANES)), near_top)
                probs = jnp.exp(scores - jnp.concatenate([top] * (2 * rows // LANES), axis=1))
                fade = jnp.exp(near_top - top)
                total = jnp.broadcast_to(jnp.sum(probs, axis=-1, keepdims=True), (32, LANES))
                total = total + u[part, lanes_at(index * pairs_e + pair, LANES)] * fade
                p_b[index, part] = probs.astype(BF)
                fade_e[index, part] = fade
                scale_e[index, part] = 1.0 / total
                stat_e[index, part] = top + jnp.log(total)
            wide = dot_nn(p_b[index], v2) + o_f[:, lanes_at(pair, LANES)] * fade_e[index]
            outs.append(wide * scale_e[index])
        lse_e[pair] = jnp.where(low_lane, stat_e[0], stat_e[1])
        both = jnp.where(low_lane, outs[0], outs[1])
        o_f[:, lanes_at(pair, LANES)] = both
        o_b[:, lanes_at(pair, LANES)] = both.astype(BF)

    key_values(0, 2)
    each(pairs_e, UNROLL["attend"], near_pair)
    key_values(2, 4)
    sends.extend(forward(block) for block in range(blocks))
    each(pairs_e, UNROLL["attend"], far_pair)
    load_o.wait()

    def out_cols(at):
        h1[:, at] = x0[:, at] + dot_nn(o_b[...], w_o[:, at])

    tiles(width // 256, 256, out_cols)

    def norm_two(at):
        nb[at] = rms(h1[at], gain[1]).astype(BF)

    tiles(rows // 64, 64, norm_two)
    load_1.wait()

    def hidden(at):
        value = dot_nn(nb[...], w_1[:, at])
        u[:, at] = value
        act[:, at] = gelu(value).astype(BF)

    tiles(u.shape[1] // 256, 256, hidden)
    load_2.wait()

    def hidden_out(at):
        h2[:, at] = h1[:, at] + dot_nn(act[...], w_2[:, at])

    tiles(width // 256, 256, hidden_out)

    def norm_out(at):
        eo[head, at] = rms(h2[at], gain[2]).astype(BF)

    tiles(rows // 64, 64, norm_out)
    got_e = send(6, eo.at[head], eo.at[head], to_mate)
    load_ckv.wait()

    def cross_keys(slot):
        def body(at):
            ckv[slot, :, at] = dot_nn(eo[slot], w_ckv[:, at]).astype(BF)

        tiles(2 * own // 256, 256, body)

    cross_keys(head)
    got_e.wait_recv()
    cross_keys(mate)


    def cross_pair(pair):
        k2 = ckv[:, :, lanes_at(pair, LANES)].reshape(2 * rows, LANES)
        v2 = ckv[:, :, lanes_at(pair, LANES, own)].reshape(2 * rows, LANES)
        return cq[:, lanes_at(pair, LANES)], k2, v2

    st_p[...] = jnp.zeros_like(st_p)

    def cross_attend(pair):
        q2, k2, v2 = cross_pair(pair)
        stats = st_p[...]
        outs = []
        for index, side in enumerate(sides):
            scores = jnp.where(okc, dot_nt(q2 * side, k2), NEG)
            top = jnp.max(scores, axis=-1, keepdims=True)
            probs = jnp.exp(scores - top)
            total = jnp.sum(probs, axis=-1, keepdims=True)
            outs.append(dot_nn(probs.astype(BF), v2) / total)
            stats = jnp.where(lane == 2 * pair + index, top + jnp.log(total), stats)
        both = jnp.where(low_lane, outs[0], outs[1])
        cp[:, lanes_at(pair, LANES)] = both
        cp_b[:, lanes_at(pair, LANES)] = both.astype(BF)
        st_p[...] = stats

    each(pairs_d, UNROLL["cross"], cross_attend)
    mine_t = pl.ds(pl.multiple_of(chip * half, half), half)
    theirs_t = pl.ds(pl.multiple_of(across * half, half), half)
    got_c = send(7, cp_b.at[theirs_t], co_r, to_across)
    got_s = send(8, st_p.at[theirs_t], st_r, to_across)
    got_c.wait_recv()
    got_s.wait_recv()
    l_own, l_oth = st_p[mine_t], st_r[...]
    top = jnp.maximum(l_own, l_oth)
    lse_c = top + jnp.log(jnp.exp(l_own - top) + jnp.exp(l_oth - top))
    w_own, w_oth = jnp.exp(l_own - lse_c), jnp.exp(l_oth - lse_c)

    def side_cols(array, pair):
        return jnp.where(
            low_lane, array[:, 2 * pair : 2 * pair + 1], array[:, 2 * pair + 1 : 2 * pair + 2]
        )

    for pair in range(pairs_d):
        lo = pair * LANES
        both = cp[mine_t, lo : lo + LANES] * side_cols(w_own, pair)
        both = both + co_r[:, lo : lo + LANES].astype(F32) * side_cols(w_oth, pair)
        co[:, lo : lo + LANES] = both
        co_b[:, lo : lo + LANES] = both.astype(BF)

    def exchange(index, value):
        slot = index - 9
        px_s[slot] = value.astype(BF)
        got = send(index, px_s.at[slot], px_r.at[slot], to_mate)
        got.wait_recv()
        return px_s[slot].astype(F32) + px_r[slot].astype(F32)

    load_co.wait()
    a2[...] = a1[mine_t] + exchange(9, dot_nn(co_b[...], w_co[...]))
    m_b[0:half] = rms(a2[...], gain[5]).astype(BF)
    load_d1.wait()

    def dec_hidden(at):
        value = dot_nn(m_b[0:half], w_d1[:, at])
        du[:, at] = value
        dact[:, at] = gelu(value).astype(BF)

    tiles(du.shape[1] // 512, 512, dec_hidden)
    load_d2.wait()
    a3[...] = a2[...] + exchange(10, dot_nn(dact[...], w_d2[...]))
    f_b[...] = rms(a3[...], gain[6]).astype(BF)

    acc[...] = jnp.zeros_like(acc)

    def vocab_step(logits, table, top, total):
        new_top = jnp.maximum(top, jnp.max(logits, axis=-1, keepdims=True))
        fade = jnp.exp(top - new_top)
        probs = jnp.exp(logits - new_top)
        acc[...] = acc[...] * fade + dot_nn(probs.astype(BF), table)
        return new_top, total * fade + jnp.sum(probs, axis=-1, keepdims=True)

    def refill(index, slot):
        @pl.when(index + RING < full)
        def _():
            chunk_copy(index + RING, slot).start()

        if tail:

            @pl.when(index + RING == full)
            def _():
                tail_copy().start()

    span = UNROLL["vocab"]
    chunk_copy(0, 0).wait()
    lg[0] = dot_nt(f_b[...], ring[0])

    def vocab_chunks(turn, carry):
        first = span * turn
        slots = [lax.rem(first + k, RING) for k in range(span + 1)]
        for k in range(span):
            chunk_copy(first + k + 1, slots[k + 1]).wait()
            lg[(k + 1) % 2] = dot_nt(f_b[...], ring[slots[k + 1]])
            carry = vocab_step(lg[k % 2], ring[slots[k]], *carry)
            refill(first + k, slots[k])
        return carry

    carry = (jnp.full((half, 1), NEG, F32), jnp.zeros((half, 1), F32))
    turns = (full - 1) // span
    carry = lax.fori_loop(0, turns, vocab_chunks, carry)
    for index in range(span * turns, full):
        slot, after = index % RING, (index + 1) % RING
        if index + 1 < full:
            chunk_copy(index + 1, after).wait()
            lg[(index + 1) % 2] = dot_nt(f_b[...], ring[after])
        elif tail:
            tail_copy().wait()
            lg[(index + 1) % 2, :, 0:tail] = dot_nt(f_b[...], ring[after, 0:tail])
        carry = vocab_step(lg[index % 2], ring[slot], *carry)
        refill(index, slot)
    if tail:
        carry = vocab_step(lg[full % 2, :, 0:tail], ring[full % RING, 0:tail], *carry)
    top, total = carry
    acc_b[...] = (acc[...] / total).astype(BF)
    vl_s[...] = jnp.broadcast_to(top + jnp.log(total), vl_s.shape)
    got_a = send(11, acc_b, acc_r, to_mate)
    got_v = send(12, vl_s, vl_r, to_mate)
    pick = jnp.sum(f_b[...].astype(F32) * tgt[...], axis=-1, keepdims=True)
    got_a.wait_recv()
    got_v.wait_recv()
    l_own, l_oth = vl_s[:, 0:1], vl_r[:, 0:1]
    top = jnp.maximum(l_own, l_oth)
    lse_v = top + jnp.log(jnp.exp(l_own - top) + jnp.exp(l_oth - top))
    loss = jnp.sum(share * (lse_v - pick), axis=0, keepdims=True) * jnp.where(head == 0, 1.0, 0.0)
    mean_row = acc_b[...].astype(F32) * jnp.exp(l_own - lse_v) + acc_r[...].astype(F32) * jnp.exp(l_oth - lse_v)
    gffn[...] = rms_grad(a3[...], gain[6], share * (mean_row - tgt[...]))

    m_b[0:half] = gffn[...].astype(BF)

    def dec_hidden_grad(at):
        value = dot_nt(m_b[0:half], w_d2[at])
        dact[:, at] = gelu_grad(du[:, at], value).astype(BF)

    tiles(du.shape[1] // 512, 512, dec_hidden_grad)
    slope = exchange(13, dot_nt(dact[...], w_d1[...]))
    gcross = gffn[...] + rms_grad(a2[...], gain[5], slope)
    gco[chip] = dot_nt(gcross.astype(BF), w_co[...]).astype(BF)
    stats = lse_c
    for pair in range(pairs_d):
        lo = pair * LANES
        value = gco[chip, :, lo : lo + LANES].astype(F32) * co[:, lo : lo + LANES]
        for index in range(2):
            picked_side = jnp.where(low_lane == (index == 0), value, 0.0)
            delta = jnp.sum(picked_side, axis=-1, keepdims=True)
            stats = jnp.where(lane == HD + 2 * pair + index, delta, stats)
    st_g[chip] = stats
    got_g = send(14, gco.at[chip], gco.at[chip], to_across)
    got_t = send(15, st_g.at[chip], st_g.at[chip], to_across)
    got_g.wait_recv()
    got_t.wait_recv()

    def cross_back(pair):
        q2, k2, v2 = cross_pair(pair)
        do2 = gco[:, :, lanes_at(pair, LANES)].reshape(all_tgt, LANES)
        stats = st_g[...].reshape(all_tgt, LANES)
        dks, dvs = [], []
        for index, side in enumerate(sides):
            column = 2 * pair + index
            lse = jnp.sum(jnp.where(lane == column, stats, 0.0), axis=-1, keepdims=True)
            delta = jnp.sum(jnp.where(lane == HD + column, stats, 0.0), axis=-1, keepdims=True)
            scores = jnp.where(okc, dot_nt(q2 * side, k2), NEG)
            probs = jnp.exp(scores - lse)
            dp = dot_nt(do2 * side, v2)
            ds = (probs * (dp - delta)).astype(BF)
            dks.append(dot_tn(ds, q2))
            dvs.append(dot_tn(probs.astype(BF), do2))
        shape = (2, rows, LANES)
        dckv[:, :, lanes_at(pair, LANES)] = jnp.where(low_lane, *dks).astype(BF).reshape(shape)
        dckv[:, :, lanes_at(pair, LANES, own)] = jnp.where(low_lane, *dvs).astype(BF).reshape(shape)

    each(pairs_d, UNROLL["cross_back"], cross_back)
    def pair_grad_mate(at):
        gp_s[:, at] = dot_nt(dckv[mate], w_ckv[at]).astype(BF)

    tiles(width // 256, 256, pair_grad_mate)
    got_p = send(16, gp_s, gp_r, to_mate)

    def pair_grad_mine(at):
        gown[:, at] = dot_nt(dckv[head], w_ckv[at])

    tiles(width // 256, 256, pair_grad_mine)
    got_p.wait_recv()

    def out_grad(at):
        value = rms_grad(h2[at], gain[2], gown[at].astype(BF).astype(F32) + gp_r[at].astype(F32))
        go[at] = value
        nb[at] = value.astype(BF)

    tiles(rows // 64, 64, out_grad)

    def hidden_grad(at):
        act[:, at] = gelu_grad(u[:, at], dot_nt(nb[...], w_2[at])).astype(BF)

    tiles(u.shape[1] // 256, 256, hidden_grad)

    def norm_two_grad(at):
        spare[:, at] = dot_nt(act[...], w_1[at])

    tiles(width // 256, 256, norm_two_grad)

    def one_grad(at):
        value = go[at] + rms_grad(h1[at], gain[1], spare[at])
        go[at] = value
        nb[at] = value.astype(BF)

    tiles(rows // 64, 64, one_grad)

    def attn_grad(at):
        d_o[:, at] = dot_nt(nb[...], w_o[at]).astype(BF)

    tiles(width // 256, 256, attn_grad)

    lead_keys = 4 * LEAD_PAD

    quad = 2 * LANES
    heads_in = quad // HD
    quad_lane = lax.broadcasted_iota(jnp.int32, (1, quad), 1)
    quad_of = [(quad_lane >= k * HD) & (quad_lane < (k + 1) * HD) for k in range(heads_in)]
    quad_b = [jnp.where(inside, 1.0, 0.0).astype(BF) for inside in quad_of]

    def lead_pair(group, part):
        pair = 2 * group + part
        at = lanes_at(pair, LANES)
        q2, do2 = q_s[:, at], d_o[:, at]
        k2 = kv[:, 0:LEAD_PAD, at].reshape(lead_keys, LANES)
        v2 = kv[:, 0:LEAD_PAD, lanes_at(pair, LANES, width)].reshape(lead_keys, LANES)
        value = do2.astype(F32) * o_f[:, at]
        dks, dvs, deltas = [], [], []
        for index, side in enumerate(sides):
            delta = jnp.sum(jnp.where(low_lane == (index == 0), value, 0.0), axis=-1, keepdims=True)
            deltas.append(delta)
            lse = lse_e[pair, :, index * HD : index * HD + 1]
            scores = jnp.where(okl, dot_nt(q2 * side, k2), NEG)
            probs = jnp.exp(scores - lse)
            ds = (probs * (dot_nt(do2 * side, v2) - delta)).astype(BF)
            dks.append(dot_tn(ds, q2))
            dvs.append(dot_tn(probs.astype(BF), do2))
        lo = part * LANES
        shape = (4, LEAD_PAD, LANES)
        dkv[group, :, :, lo : lo + LANES] = jnp.where(low_lane, *dks).astype(BF).reshape(shape)
        dkv[group, :, :, quad + lo : quad + lo + LANES] = jnp.where(low_lane, *dvs).astype(BF).reshape(shape)
        dl[pair] = jnp.where(low_lane, *[d[0:LEAD_PAD] for d in deltas])

    def stack(value):
        return jnp.concatenate([value * side for side in quad_b], axis=0)

    def column(ref, group, rows_at):
        return jnp.concatenate(
            [ref[2 * group + k // 2, rows_at, (k % 2) * HD : (k % 2) * HD + 1] for k in range(heads_in)], axis=0
        )

    def query_quad(group):
        at, vat = lanes_at(group, quad), lanes_at(group, quad, width)
        lead_rows = slice(0, LEAD_PAD)
        k4 = kv[:, :, at].reshape(keys, quad)
        v4 = kv[:, :, vat].reshape(keys, quad)
        scores = jnp.where(ok, dot_nt(stack(q_s[lead_rows, at]), k4), NEG)
        probs = jnp.exp(scores - column(lse_e, group, lead_rows))
        ds = (probs * (dot_nt(stack(d_o[lead_rows, at]), v4) - column(dl, group, lead_rows))).astype(BF)
        wide = dot_nn(ds, k4)
        value = jnp.zeros((LEAD_PAD, quad), F32)
        for k in range(heads_in):
            value = jnp.where(quad_of[k], wide[k * LEAD_PAD : (k + 1) * LEAD_PAD], value)
        gj[:, at] = (value * HD ** (-0.5)).astype(BF)

    def key_copies(group):
        plan = ((slot_across, 1, to_across), (slot_diag, 2, to_diag), (slot_mate, 0, to_mate))
        copies = []
        for k, (slot, place, peer) in enumerate(plan):
            copies.append(
                pltpu.make_async_remote_copy(
                    src_ref=dkv.at[group, slot],
                    dst_ref=dkv_r.at[group, place],
                    send_sem=send_sem.at[17 + 3 * group + k],
                    recv_sem=recv_sem.at[17 + 3 * group + k],
                    device_id=peer,
                    device_id_type=MESH,
                )
            )
        return copies

    def lead_group(group):
        lead_pair(group, 0)
        lead_pair(group, 1)
        for copy in key_copies(group):
            copy.start()

    each(width // quad, UNROLL["lead"], lead_group)
    each(width // quad, UNROLL["lead"], query_quad)
    for group in range(width // quad):
        summed = dkv[group, me].astype(F32)
        copies = key_copies(group)
        for index in range(3):
            copies[(2, 0, 1)[index]].wait_recv()
            summed = summed + dkv_r[group, index].astype(F32)
        sends.extend(copies)
        lo = group * quad
        gj[:, width + lo : width + lo + quad] = summed[:, :quad].astype(BF)
        gj[:, 2 * width + lo : 2 * width + lo + quad] = summed[:, quad:].astype(BF)

    def start_grad(at):
        spare[0:LEAD_PAD, at] = dot_nt(gj[...], w_qkv[at])

    tiles(width // 256, 256, start_grad)
    top_rows = slice(0, LEAD_PAD)
    value = go[top_rows] + rms_grad(x0[top_rows], gain[0], spare[top_rows])
    spot = lax.broadcasted_iota(jnp.int32, (LEAD_PAD, width), 0)
    extra = jnp.where(spot == leads, loss, 0.0)
    blk[...] = jnp.where(spot < leads, value, extra)

    piece = LEAD_PAD // n_grp
    fold = 16 // piece if piece < 16 else 1
    narrow = width // fold
    base = leads - leads % piece
    line_at = lax.broadcasted_iota(jnp.int32, (piece, width), 0)

    def folded(value, member):
        first = leads - base
        lines = value[first : first + 1] + value[first + 1 : first + 2] + value[first + 2 : first + 3]
        for k in range(3):
            high = lines.astype(BF).astype(F32)
            value = jnp.where((line_at == first + k) & (member * piece == base), high, value)
            lines = lines - high
        parts = [value[:, k * narrow : (k + 1) * narrow] for k in range(fold)]
        return jnp.concatenate(parts, axis=0).astype(BF) if fold > 1 else value.astype(BF)

    def unfolded(value):
        value = value.astype(F32)
        parts = [value[k * piece : (k + 1) * piece] for k in range(fold)]
        return jnp.concatenate(parts, axis=1) if fold > 1 else value

    slot = block_sem + 4 * blocks
    got = []
    for step in range(n_grp):
        member = lax.rem(grp + step, n_grp)
        rows_at = pl.ds(pl.multiple_of(member * piece, piece), piece)
        if step:
            got.append(send(slot, blk.at[rows_at], s1_r.at[step], {"grp": member}))
            slot += 1
    value = blk[pl.ds(pl.multiple_of(grp * piece, piece), piece)]
    for step in range(1, n_grp):
        got[step - 1].wait_recv()
        value = value + s1_r[step]
    s2_r[ex] = value
    got = []
    for step in range(1, n_ex):
        got.append(send(slot, s2_r.at[ex], s2_r.at[ex], ex_peer(step)))
        slot += 1
    for copy in got:
        copy.wait_recv()
    value = s2_r[0]
    for member in range(1, n_ex):
        value = value + s2_r[member]
    all_r[me, grp] = folded(value, grp)
    got = []
    for step in range(1, n_grp * QUARTERS):
        got.append(send(slot, all_r.at[me, grp], all_r.at[me, grp], plane_peer(step)))
        slot += 1
    for copy in got:
        copy.wait_recv()
    for quarter in range(QUARTERS):
        for member in range(n_grp):
            out[quarter, member * piece : (member + 1) * piece] = unfolded(all_r[quarter, member])
    for copy in sends:
        copy.wait_send()


def main_call(lengths, vmem, hbm):
    half = vmem[1].shape[1] // 2
    rows = (hbm[0].shape[0] - 3 * half) // 2
    wq, wo, w1, w2, dqkv, dwo, cqw, ckvw, cwo, dw1, dw2, emb = hbm[1:]
    width, own, ff, dff, tgt_all = wo.shape[0], dwo.shape[0], w1.shape[1], dw1.shape[1], 2 * half
    pairs_e = width // LANES

    def v(shape, kind=F32):
        return pltpu.VMEM(shape, kind)

    scratch = [v(w.shape, BF) for w in hbm[1:12]]
    scratch += [v((RING, CHUNK, width), BF)]
    scratch += [v((64, width))]
    scratch += [v((rows, width), BF), v((rows, width), BF), v((tgt_all + half, width), BF), v((tgt_all + half, width), BF)]
    scratch += [v((rows, width)) for _ in range(5)]
    scratch += [v((4, rows, width), BF), v((rows, width), BF), v((4, rows, 2 * width), BF)]
    scratch += [v((rows, width)), v((rows, width), BF), v((2, rows, 2 * rows)), v((2, rows, 2 * rows), BF)]
    scratch += [v((pairs_e, rows, LANES))]
    scratch += [v((2, rows, LANES)), v((2, rows, LANES)), v((2, rows, LANES)), v((rows, width), BF)]
    scratch += [v((rows, ff)), v((rows, ff), BF)]
    scratch += [v((2, rows, width), BF), v((2, rows, 2 * own), BF), v((2, rows, 2 * own), BF)]
    scratch += [v((rows, width), BF), v((rows, width), BF), v((rows, width)), v((rows, width), BF)]
    groups = width // (2 * LANES)
    scratch += [v((groups, 4, LEAD_PAD, 4 * LANES), BF), v((groups, 3, LEAD_PAD, 4 * LANES), BF), v((LEAD_PAD, 3 * width), BF)]
    scratch += [v((pairs_e, LEAD_PAD, LANES))]
    scratch += [v((tgt_all, width)), v((tgt_all, width)), v((tgt_all, width), BF), v((tgt_all, 3 * own), BF)]
    scratch += [v((tgt_all, own), BF), v((tgt_all, width), BF), v((tgt_all, width), BF), v((tgt_all, own), BF)]
    scratch += [v((tgt_all, own)), v((tgt_all, own), BF), v((tgt_all, LANES)), v((half, LANES))]
    scratch += [v((half, own), BF), v((half, own)), v((half, own), BF)]
    scratch += [v((2, half, CHUNK))]
    scratch += [v((5, half, width), BF), v((5, half, width), BF)]
    scratch += [v((half, width)), v((half, width)), v((half, dff)), v((half, dff), BF), v((half, width), BF)]
    scratch += [v((half, width)), v((half, width)), v((half, width), BF), v((half, width), BF)]
    scratch += [v((half, LANES)), v((half, LANES)), v((half, width)), v((2, half, own), BF), v((2, half, LANES))]
    n_grp, n_ex = lax.axis_size("grp"), lax.axis_size("ex")
    piece = LEAD_PAD // n_grp
    fold = 16 // piece if piece < 16 else 1
    folded = (piece * fold, width // fold)
    scratch += [v((LEAD_PAD, width)), v((n_grp, piece, width)), v((n_ex, piece, width))]
    scratch += [v((QUARTERS, n_grp, *folded), BF)]
    exchanges = 17 + 3 * groups + 4 * (rows // 64) + (n_grp - 1) + (n_ex - 1) + (n_grp * QUARTERS - 1)
    scratch += [
        pltpu.SemaphoreType.DMA((13,)),
        pltpu.SemaphoreType.DMA((RING,)),
        pltpu.SemaphoreType.DMA((exchanges,)),
        pltpu.SemaphoreType.DMA((exchanges,)),
    ]
    any_spec, vmem_spec = pl.BlockSpec(memory_space=pl.ANY), pl.BlockSpec(memory_space=pltpu.VMEM)
    return pl.pallas_call(
        main_kernel,
        out_shape=jax.ShapeDtypeStruct((QUARTERS, LEAD_PAD, width), F32),
        in_specs=[pl.BlockSpec(memory_space=pltpu.SMEM), any_spec] + [vmem_spec] * len(vmem) + [any_spec] * len(hbm[1:]),
        out_specs=vmem_spec,
        scratch_shapes=scratch,
        compiler_params=pltpu.CompilerParams(
            collective_id=1, has_side_effects=True, vmem_limit_bytes=62 * 1024 * 1024
        ),
        name="step_of_one_example",
    )(lengths, hbm[0], *vmem, *hbm[1:])


def log2(size):
    return size.bit_length() - 1


def ids_kernel(enc_ids, dec_ids, target_ids, out, lines, got, unused, send_sem, recv_sem):
    ex, chip = lax.axis_index("ex"), lax.axis_index("chip")
    chips = lax.axis_size("chip")
    seqs = lax.axis_size(SEQ)
    me = ex * chips + chip
    enc_dev, tgt_dev = enc_ids.shape[1], dec_ids.shape[1]


    def peer_of(step):
        peer = lax.rem(me + step, seqs)
        row = lax.div(peer, chips)
        return row, {"ex": row, "chip": peer - row * chips}

    barrier = pltpu.get_barrier_semaphore()
    for step in range(1, seqs):
        pl.semaphore_signal(barrier, inc=1, device_id=peer_of(step)[1], device_id_type=MESH)
    lines[:, 0:enc_dev] = enc_ids[...]
    lines[:, enc_dev : enc_dev + tgt_dev] = dec_ids[...]
    lines[:, enc_dev + tgt_dev : enc_dev + 2 * tgt_dev] = target_ids[...]
    lines[:, enc_dev + 2 * tgt_dev :] = jnp.zeros((lines.shape[0], lines.shape[1] - enc_dev - 2 * tgt_dev), jnp.int32)
    pl.semaphore_wait(barrier, seqs - 1)

    for step in range(1, seqs):
        row, peer = peer_of(step)
        pltpu.make_async_remote_copy(
            src_ref=lines.at[pl.ds(row, 1)],
            dst_ref=got.at[pl.ds(me, 1)],
            send_sem=send_sem,
            recv_sem=recv_sem,
            device_id=peer,
            device_id_type=MESH,
        ).start()
    own_line = lines.at[pl.ds(ex, 1)]
    pltpu.make_async_copy(own_line, got.at[pl.ds(me, 1)], recv_sem).start()
    pltpu.make_async_copy(own_line, unused.at[pl.ds(0, 1)], send_sem).start()
    pltpu.make_async_copy(got, got, recv_sem).wait()
    pltpu.make_async_copy(got, got, send_sem).wait()
    out[...] = got[...]


def ids_call(enc_ids, dec_ids, target_ids):
    seqs = lax.axis_size(SEQ)
    lanes = -(-(enc_ids.shape[1] + 2 * dec_ids.shape[1]) // LANES) * LANES
    return pl.pallas_call(
        ids_kernel,
        out_shape=jax.ShapeDtypeStruct((seqs, lanes), jnp.int32),
        in_specs=[pl.BlockSpec(memory_space=pltpu.VMEM)] * 3,
        out_specs=pl.BlockSpec(memory_space=pltpu.VMEM),
        scratch_shapes=[
            pltpu.VMEM((enc_ids.shape[0], lanes), jnp.int32),
            pltpu.VMEM((seqs, lanes), jnp.int32),
            pltpu.VMEM((8, lanes), jnp.int32),
            pltpu.SemaphoreType.DMA,
            pltpu.SemaphoreType.DMA,
        ],
        compiler_params=pltpu.CompilerParams(collective_id=2, has_side_effects=True),
        name="ids_of_one_example",
    )(enc_ids, dec_ids, target_ids)


GROUP = 16


AHEAD = 8


def lookup_kernel(rows, tokens, lead, enc_dev, tgt_dev, ids, table, out, blocks, spots, sems):
    chip, head = lax.axis_index("chip"), lax.axis_index("head")
    vocab_part = table.shape[0]
    enc_count = 2 * rows
    tgt_all = tgt_dev * ids.shape[0]
    half = tgt_all // 2
    groups = out.shape[0] // GROUP
    first, second = enc_count // GROUP, (enc_count + tgt_all) // GROUP

    def fetch(group):
        enc = group < first
        slot = (group * GROUP) >> log2(rows)
        enc_base = (PROMPT - lead) + tokens * (2 * chip + slot) + ((group * GROUP) & (rows - 1))
        dec_base = (group - jnp.where(group < second, first, second)) * GROUP
        dec_base = dec_base + jnp.where(group < second, 0, chip * half)
        base = jnp.where(enc, enc_base, dec_base)
        shift = jnp.where(enc, log2(enc_dev), log2(tgt_dev))
        mask = jnp.where(enc, enc_dev - 1, tgt_dev - 1)
        lane = jnp.where(enc, 0, jnp.where(group < second, enc_dev, enc_dev + tgt_dev))
        for k in range(GROUP):
            token = ids[(base + k) >> shift, lane + ((base + k) & mask)]
            upper = jnp.where(token >= vocab_part, 1, 0)
            local = token - upper * vocab_part
            spots[group * GROUP + k] = k * GROUP + (local & (GROUP - 1)) + ((upper + head - 2 * upper * head) * 4096)
            at = pl.multiple_of((local >> log2(GROUP)) << log2(GROUP), GROUP)
            pltpu.make_async_copy(
                table.at[pl.ds(at, GROUP)], blocks.at[group * GROUP + k], sems.at[group]
            ).start()

    across = lax.broadcasted_iota(jnp.int32, (8, LANES), 1)
    down = lax.broadcasted_iota(jnp.int32, (8, LANES), 0)

    def select(group):
        at = pl.ds(pl.multiple_of(group * GROUP, GROUP), GROUP)
        pltpu.make_async_copy(blocks.at[at], blocks.at[at], sems.at[group]).wait()
        chosen = []
        for part in range(GROUP // 8):
            want = jnp.full((8, LANES), -1, jnp.int32)
            for k in range(8):
                want = jnp.where(down == k, spots[group * GROUP + part * 8 + k], want)
            hits = [jnp.where(across + base == want, 1.0, 0.0) for base in range(0, GROUP * GROUP, LANES)]
            chosen.append(jnp.concatenate(hits, axis=1))
        chosen = jnp.concatenate(chosen, axis=0).astype(BF)
        out[at] = dot_nn(chosen, blocks[at].reshape(GROUP * GROUP, out.shape[1])).astype(BF)

    def loop(start, stop, *steps):
        def body(group, carry):
            for step in steps:
                step(group)
            return carry

        lax.fori_loop(start, stop, body, 0)

    loop(0, AHEAD, fetch)
    loop(AHEAD, groups, fetch, lambda group: select(group - AHEAD))
    loop(groups - AHEAD, groups, select)


def lookup_call(ids, table, rows, tokens, lead, enc_dev, tgt_dev):
    count = 2 * rows + tgt_dev * ids.shape[0] * 3 // 2
    width = table.shape[1]
    return pl.pallas_call(
        functools.partial(lookup_kernel, rows, tokens, lead, enc_dev, tgt_dev),
        out_shape=jax.ShapeDtypeStruct((count, width), BF),
        in_specs=[pl.BlockSpec(memory_space=pltpu.SMEM), pl.BlockSpec(memory_space=pl.ANY)],
        out_specs=pl.BlockSpec(memory_space=pltpu.VMEM),
        scratch_shapes=[
            pltpu.VMEM((count, GROUP, width), BF),
            pltpu.SMEM((count,), jnp.int32),
            pltpu.SemaphoreType.DMA((count // GROUP,)),
        ],
        compiler_params=pltpu.CompilerParams(vmem_limit_bytes=32 * 1024 * 1024),
        name="embedding_rows",
    )(ids, table)


def lamb_kernel(summed, first_old, second_old, prompt, loss, grad_norm, norms, first_new, second_new, prompt_new, work):
    lead = PROMPT // QUARTERS
    for quarter in range(QUARTERS):
        work[quarter * lead : (quarter + 1) * lead] = summed[quarter, 0:lead]
    grad = work[...]
    total = summed[0, lead : lead + 3, 0:1]
    for quarter in range(1, QUARTERS):
        total = total + summed[quarter, lead : lead + 3, 0:1]
    loss[0] = jnp.sum(total)
    norm = jnp.sqrt(jnp.sum(grad * grad))
    grad_norm[0] = norm
    clipped = grad * (clip_bound / jnp.maximum(norm, clip_bound))
    first_next = beta_first * first_old[...] + (1.0 - beta_first) * clipped
    second_next = beta_second * second_old[...] + (1.0 - beta_second) * clipped * clipped
    first_new[...] = first_next
    second_new[...] = second_next
    scaled_first = first_next / (1.0 - beta_first**STEP)
    scaled_second = second_next / (1.0 - beta_second**STEP)
    param = prompt[...]
    update = scaled_first / (jnp.sqrt(scaled_second) + adam_eps) + decay_rate * param
    param_norm = jnp.sqrt(jnp.sum(param * param))
    update_norm = jnp.sqrt(jnp.sum(update * update))
    norms[0] = param_norm
    norms[1] = update_norm
    prompt_new[...] = param - learn_rate * (param_norm / update_norm) * update


def lamb_call(summed, first_old, second_old, prompt):
    smem, vmem = pl.BlockSpec(memory_space=pltpu.SMEM), pl.BlockSpec(memory_space=pltpu.VMEM)
    like = jax.ShapeDtypeStruct(prompt.shape, F32)
    return pl.pallas_call(
        lamb_kernel,
        out_shape=(
            jax.ShapeDtypeStruct((1,), F32),
            jax.ShapeDtypeStruct((1,), F32),
            jax.ShapeDtypeStruct((2,), F32),
            like,
            like,
            like,
        ),
        in_specs=[vmem] * 4,
        out_specs=(smem, smem, smem, vmem, vmem, vmem),
        scratch_shapes=[pltpu.VMEM(prompt.shape, F32)],
        name="lamb",
    )(summed, first_old, second_old, prompt)


def shards(
    enc_ids,
    lengths,
    dec_ids,
    target_ids,
    loss_mask,
    embedding,
    prompt,
    first_moment,
    second_moment,
    gains,
    enc_qkv,
    enc_wo,
    enc_w1,
    enc_w2,
    dec_qkv,
    dec_wo,
    cross_q,
    cross_kv,
    cross_wo,
    dec_w1,
    dec_w2,
):
    width = embedding.shape[1]
    own = dec_wo.shape[0]
    enc_dev, tgt_dev = enc_ids.shape[1], dec_ids.shape[1]
    total_len = enc_dev * lax.axis_size(SEQ)
    lead = PROMPT // QUARTERS
    tokens = (total_len - PROMPT) // QUARTERS
    rows = total_len // QUARTERS
    ids = ids_call(enc_ids, dec_ids, target_ids)
    picked = lookup_call(ids, embedding, rows, tokens, lead, enc_dev, tgt_dev)
    summed = main_call(
        lengths,
        (prompt, loss_mask, gains),
        (
            picked,
            enc_qkv,
            enc_wo,
            enc_w1,
            enc_w2,
            jnp.transpose(dec_qkv, (1, 0, 2)),
            dec_wo,
            cross_q,
            cross_kv.reshape(width, 2 * own),
            cross_wo,
            dec_w1,
            dec_w2,
            embedding,
        ),
    )
    loss, grad_norm, norms, first_new, second_new, prompt_new = lamb_call(summed, first_moment, second_moment, prompt)
    return loss.reshape(()), grad_norm.reshape(()), norms, first_new, second_new, prompt_new


def solution(mesh):
    finer = Mesh(
        mesh.devices.reshape(mesh.shape["grp"], mesh.shape["seq"] // 2, 2, mesh.shape["head"]),
        ("grp", "ex", "chip", "head"),
    )
    placed = (
        P("grp", SEQ),
        P("grp"),
        P("grp", SEQ),
        P("grp", SEQ),
        P("grp", None),
        P("head", None),
        P(),
        P(),
        P(),
        P(),
        P(),
        P(),
        P(),
        P(),
        P(None, None, "head"),
        P("head", None),
        P(None, "head"),
        P(None, None, "head"),
        P("head", None),
        P(None, "head"),
        P("head", None),
    )
    return jax.shard_map(
        shards,
        mesh=finer,
        in_specs=placed,
        out_specs=(P(), P(), P(), P(), P(), P()),
        check_vma=False,
    )
```

profile of v0, /device:TPU:1, one launch (start us, length us, event | category | flops | bytes accessed | tf_op | source)
XLA Modules:
  0.0 131.5 jit_solution(3381306919540903495)
XLA Ops:
  0.6 11.5 %ids_of_one_example.1.ids = s32[16,128]{1,0:T(8,128)} custom-call(s32[8,64]{1,0:T(8,128)} %enc_ids.1, s32[8,8]{1,0:T(8,128)} %dec_ids.1, s32[8,8]{1,0:T(8,128)} %target_ids.1), custom_call_target="tpu_custom_call" | custom-call | tf_op jit(solution)/shard_map/ids_of_one_example/pallas_call | solution.py:926
  12.1 0.0 copy-start.1
  12.1 0.7 copy-done.1
  12.8 0.0 copy-start.2
  12.8 13.8 %embedding_rows.1.picked = bf16[704,768]{1,0:T(8,128)(2,1)S(1)} custom-call(s32[16,128]{1,0:T(8,128)S(1)} %copy-done.1, bf16[16064,768]{1,0:T(8,128)(2,1)} %embedding.1), custom_call_target="tpu_custom_call" | custom-call | tf_op jit(solution)/shard_map/embedding_rows/pallas_call | solution.py:1010
  26.6 0.0 copy-start
  26.6 1.0 copy-done
  27.6 0.0 copy-done.2
  27.6 1.3 copy.27
  28.8 99.5 %step_of_one_example.1.summed = f32[4,32,768]{2,1,0:T(8,128)} custom-call(s32[8]{0:T(128)} %lengths.1, bf16[704,768]{1,0:T(8,128)(2,1)} %copy-done, f32[100,768]{1,0:T(8,128)} %prompt.3, s32[8,128]{1,0:T(8,128)} %loss_mask.1, f32[7,768]{1,0:T(8,128)} %gains.1, bf16[768,2304]{1,0:T(8,128)(2,1)} %enc_qkv.1, bf16[768,768]{1,0:T(8,128)(2,1)} %enc_wo.1, ...), custom_call_target="tpu_custom_call" | custom-call | tf_op jit(solution)/shard_map/step_of_one_example/pallas_call | solution.py:866
  128.3 3.0 %lamb.1 = (f32[1]{0:T(128)}, f32[1]{0:T(128)}, f32[2]{0:T(128)}, f32[100,768]{1,0:T(8,128)}, f32[100,768]{1,0:T(8,128)}, /*index=5*/f32[100,768]{1,0:T(8,128)}) custom-call(f32[4,32,768]{2,1,0:T(8,128)} %step_of_one_example.1.summed, f32[100,768]{1,0:T(8,128)} %first_old.1, f32[100,768]{1,0:T(8,128)} %second_old.1, f32[100,768]{1,0:T(8,128)} %prompt.3), custom_call_target="tpu_custom_call" | custom-call | tf_op jit(solution)/shard_map/lamb/pallas_call | solution.py:1055
Async XLA Ops:
  12.1 0.7 copy-start.1
  12.8 14.8 %copy-start.2 = (bf16[768,2,384]{2,1,0:T(2,128)(2,1)S(1)}, bf16[768,2,384]{2,1,0:T(2,128)(2,1)}, u32[]{:S(2)}) copy-start(bf16[768,2,384]{2,1,0:T(2,128)(2,1)} %param.38) | copy-start | bytes 3538948
  26.6 1.0 copy-start
where the time goes:
time: 132 us; the launch traced here: 131 us
  Pallas kernels  128 us (97%)
  local copies, waits for them, and re-layouts  2.95 us (2%)
    pallas_call x1, Pallas kernels, main_call(): pl.pallas_call(main_kernel, out_shape=jax.ShapeDtypeStruct((QUARTERS, LEA...  99.5 us
    pallas_call x1, Pallas kernels, lookup_call(): pl.pallas_call(functools.partial(lookup_kernel, rows, tokens, lead, enc_d...  13.8 us
    pallas_call x1, Pallas kernels, ids_call(): pl.pallas_call(ids_kernel, out_shape=jax.ShapeDtypeStruct((seqs, lanes),...  11.5 us
    pallas_call x1, Pallas kernels, lamb_call(): pl.pallas_call(lamb_kernel, out_shape=(jax.ShapeDtypeStruct((1,), F32), j...  2.98 us
    unnamed x7, local copies, waits for them, and re-layouts  2.95 us

commit v1 on v0

--- a/solution.py
+++ b/solution.py
@@ -66,11 +66,10 @@
     return 0.5 * value * (1.0 + jnp.tanh(GELU_A * (value + GELU_B * (value * value * value))))
 
 
-def gelu_grad(value, grad):
+def gelu_slope(value):
     square = value * value
     bend = jnp.tanh(GELU_A * (value + GELU_B * (square * value)))
-    slope = 0.5 * (1.0 + bend) + 0.5 * value * (1.0 - bend * bend) * (GELU_A * (1.0 + 3.0 * GELU_B * square))
-    return grad * slope
+    return 0.5 * (1.0 + bend) + 0.5 * value * (1.0 - bend * bend) * (GELU_A * (1.0 + 3.0 * GELU_B * square))
 
 
 def tiles(count, size, body):
@@ -96,7 +95,7 @@
     return pl.ds(pl.multiple_of(base + index * size, LANES), size)
 
 
-UNROLL = {"attend": 1, "self": 1, "cross": 1, "cross_back": 1, "lead": 1, "vocab": 2}
+UNROLL = {"attend": 1, "self": 1, "cross": 3, "cross_back": 3, "lead": 1, "vocab": 2}
 
 
 def main_kernel(
@@ -470,6 +469,17 @@
     theirs_t = pl.ds(pl.multiple_of(across * half, half), half)
     got_c = send(7, cp_b.at[theirs_t], co_r, to_across)
     got_s = send(8, st_p.at[theirs_t], st_r, to_across)
+    ff_tiles = u.shape[1] // 256
+
+    def slopes(first, last):
+        def some_cols(index, carry):
+            at = pl.ds(pl.multiple_of(index * 256, 256), 256)
+            u[:, at] = gelu_slope(u[:, at])
+            return carry
+
+        lax.fori_loop(first, last, some_cols, 0)
+
+    slopes(0, ff_tiles // 2)
     got_c.wait_recv()
     got_s.wait_recv()
     l_own, l_oth = st_p[mine_t], st_r[...]
@@ -489,10 +499,12 @@
         co[:, lo : lo + LANES] = both
         co_b[:, lo : lo + LANES] = both.astype(BF)
 
-    def exchange(index, value):
+    def exchange(index, value, meanwhile=None):
         slot = index - 9
         px_s[slot] = value.astype(BF)
         got = send(index, px_s.at[slot], px_r.at[slot], to_mate)
+        if meanwhile is not None:
+            meanwhile()
         got.wait_recv()
         return px_s[slot].astype(F32) + px_r[slot].astype(F32)
 
@@ -508,7 +520,11 @@
 
     tiles(du.shape[1] // 512, 512, dec_hidden)
     load_d2.wait()
-    a3[...] = a2[...] + exchange(10, dot_nn(dact[...], w_d2[...]))
+
+    def dec_slope():
+        du[...] = gelu_slope(du[...])
+
+    a3[...] = a2[...] + exchange(10, dot_nn(dact[...], w_d2[...]), dec_slope)
     f_b[...] = rms(a3[...], gain[6]).astype(BF)
 
     acc[...] = jnp.zeros_like(acc)
@@ -579,7 +595,7 @@
 
     def dec_hidden_grad(at):
         value = dot_nt(m_b[0:half], w_d2[at])
-        dact[:, at] = gelu_grad(du[:, at], value).astype(BF)
+        dact[:, at] = (du[:, at] * value).astype(BF)
 
     tiles(du.shape[1] // 512, 512, dec_hidden_grad)
     slope = exchange(13, dot_nt(dact[...], w_d1[...]))
@@ -596,6 +612,7 @@
     st_g[chip] = stats
     got_g = send(14, gco.at[chip], gco.at[chip], to_across)
     got_t = send(15, st_g.at[chip], st_g.at[chip], to_across)
+    slopes(ff_tiles // 2, ff_tiles)
     got_g.wait_recv()
     got_t.wait_recv()
 
@@ -639,7 +656,7 @@
     tiles(rows // 64, 64, out_grad)
 
     def hidden_grad(at):
-        act[:, at] = gelu_grad(u[:, at], dot_nt(nb[...], w_2[at])).astype(BF)
+        act[:, at] = (u[:, at] * dot_nt(nb[...], w_2[at])).astype(BF)
 
     tiles(u.shape[1] // 256, 256, hidden_grad)
 
@@ -759,26 +776,6 @@
     blk[...] = jnp.where(spot < leads, value, extra)
 
     piece = LEAD_PAD // n_grp
-    fold = 16 // piece if piece < 16 else 1
-    narrow = width // fold
-    base = leads - leads % piece
-    line_at = lax.broadcasted_iota(jnp.int32, (piece, width), 0)
-
-    def folded(value, member):
-        first = leads - base
-        lines = value[first : first + 1] + value[first + 1 : first + 2] + value[first + 2 : first + 3]
-        for k in range(3):
-            high = lines.astype(BF).astype(F32)
-            value = jnp.where((line_at == first + k) & (member * piece == base), high, value)
-            lines = lines - high
-        parts = [value[:, k * narrow : (k + 1) * narrow] for k in range(fold)]
-        return jnp.concatenate(parts, axis=0).astype(BF) if fold > 1 else value.astype(BF)
-
-    def unfolded(value):
-        value = value.astype(F32)
-        parts = [value[k * piece : (k + 1) * piece] for k in range(fold)]
-        return jnp.concatenate(parts, axis=1) if fold > 1 else value
-
     slot = block_sem + 4 * blocks
     got = []
     for step in range(n_grp):
@@ -801,16 +798,14 @@
     value = s2_r[0]
     for member in range(1, n_ex):
         value = value + s2_r[member]
-    all_r[me, grp] = folded(value, grp)
+    all_r[me, grp] = value
     got = []
     for step in range(1, n_grp * QUARTERS):
         got.append(send(slot, all_r.at[me, grp], all_r.at[me, grp], plane_peer(step)))
         slot += 1
     for copy in got:
         copy.wait_recv()
-    for quarter in range(QUARTERS):
-        for member in range(n_grp):
-            out[quarter, member * piece : (member + 1) * piece] = unfolded(all_r[quarter, member])
+    out[...] = all_r[...].reshape(out.shape)
     for copy in sends:
         copy.wait_send()
 
@@ -851,10 +846,8 @@
     scratch += [v((half, LANES)), v((half, LANES)), v((half, width)), v((2, half, own), BF), v((2, half, LANES))]
     n_grp, n_ex = lax.axis_size("grp"), lax.axis_size("ex")
     piece = LEAD_PAD // n_grp
-    fold = 16 // piece if piece < 16 else 1
-    folded = (piece * fold, width // fold)
     scratch += [v((LEAD_PAD, width)), v((n_grp, piece, width)), v((n_ex, piece, width))]
-    scratch += [v((QUARTERS, n_grp, *folded), BF)]
+    scratch += [v((QUARTERS, n_grp, piece, width))]
     exchanges = 17 + 3 * groups + 4 * (rows // 64) + (n_grp - 1) + (n_ex - 1) + (n_grp * QUARTERS - 1)
     scratch += [
         pltpu.SemaphoreType.DMA((13,)),
@@ -997,11 +990,18 @@
                 step(group)
             return carry
 
-        lax.fori_loop(start, stop, body, 0)
-
-    loop(0, AHEAD, fetch)
-    loop(AHEAD, groups, fetch, lambda group: select(group - AHEAD))
-    loop(groups - AHEAD, groups, select)
+        lax.fori_loop(start, stop, body, 0, unroll=2 if len(steps) > 1 and (stop - start) % 2 == 0 else 1)
+
+    skip = lead // GROUP
+    per_slot = rows // GROUP - skip
+    needed = groups - 2 * skip
+
+    def real(index):
+        return index + skip + jnp.where(index >= per_slot, skip, 0)
+
+    loop(0, AHEAD, lambda index: fetch(real(index)))
+    loop(AHEAD, needed, lambda index: fetch(real(index)), lambda index: select(real(index - AHEAD)))
+    loop(needed - AHEAD, needed, lambda index: select(real(index)))
 
 
 def lookup_call(ids, table, rows, tokens, lead, enc_dev, tgt_dev):
@@ -1027,9 +1027,9 @@
     for quarter in range(QUARTERS):
         work[quarter * lead : (quarter + 1) * lead] = summed[quarter, 0:lead]
     grad = work[...]
-    total = summed[0, lead : lead + 3, 0:1]
+    total = summed[0, lead : lead + 1, 0:1]
     for quarter in range(1, QUARTERS):
-        total = total + summed[quarter, lead : lead + 3, 0:1]
+        total = total + summed[quarter, lead : lead + 1, 0:1]
     loss[0] = jnp.sum(total)
     norm = jnp.sqrt(jnp.sum(grad * grad))
     grad_norm[0] = norm

time: 132 us -> 129 us (0.977)
  Pallas kernels: 128 us -> 125 us
    pallas_call x1, Pallas kernels: 13.8 us -> 12 us  [lookup_call(): pl.pallas_call(functools.partial(lookup_kernel, rows, tokens, lead, enc_d...]
where the time goes in v1:
time: 129 us
  Pallas kernels  125 us (97%)
  local copies, waits for them, and re-layouts  2.95 us (2%)
    pallas_call x1, Pallas kernels, main_call(): pl.pallas_call(main_kernel, out_shape=jax.ShapeDtypeStruct((QUARTERS, LEA...  98.3 us
    pallas_call x1, Pallas kernels, lookup_call(): pl.pallas_call(functools.partial(lookup_kernel, rows, tokens, lead, enc_d...  12 us
    pallas_call x1, Pallas kernels, ids_call(): pl.pallas_call(ids_kernel, out_shape=jax.ShapeDtypeStruct((seqs, lanes),...  11.5 us
    pallas_call x1, Pallas kernels, lamb_call(): pl.pallas_call(lamb_kernel, out_shape=(jax.ShapeDtypeStruct((1,), F32), j...  2.98 us
    unnamed x7, local copies, waits for them, and re-layouts  2.95 us

profile of v1, /device:TPU:1, one launch (start us, length us, event | category | flops | bytes accessed | tf_op | source)
XLA Modules:
  0.0 128.5 jit_solution(876403099451345527)
XLA Ops:
  0.6 11.5 %ids_of_one_example.1.ids = s32[16,128]{1,0:T(8,128)} custom-call(s32[8,64]{1,0:T(8,128)} %enc_ids.1, s32[8,8]{1,0:T(8,128)} %dec_ids.1, s32[8,8]{1,0:T(8,128)} %target_ids.1), custom_call_target="tpu_custom_call" | custom-call | tf_op jit(solution)/shard_map/ids_of_one_example/pallas_call | solution.py:919
  12.1 0.0 copy-start.1
  12.1 0.7 copy-done.1
  12.8 0.0 copy-start.2
  12.8 12.0 %embedding_rows.1.picked = bf16[704,768]{1,0:T(8,128)(2,1)S(1)} custom-call(s32[16,128]{1,0:T(8,128)S(1)} %copy-done.1, bf16[16064,768]{1,0:T(8,128)(2,1)} %embedding.1), custom_call_target="tpu_custom_call" | custom-call | tf_op jit(solution)/shard_map/embedding_rows/pallas_call | solution.py:1010
  24.8 0.0 copy-start
  24.8 1.0 copy-done
  25.8 0.0 copy-done.2
  25.8 1.3 copy.27
  27.1 98.3 %step_of_one_example.1.summed = f32[4,32,768]{2,1,0:T(8,128)} custom-call(s32[8]{0:T(128)} %lengths.1, bf16[704,768]{1,0:T(8,128)(2,1)} %copy-done, f32[100,768]{1,0:T(8,128)} %prompt.3, s32[8,128]{1,0:T(8,128)} %loss_mask.1, f32[7,768]{1,0:T(8,128)} %gains.1, bf16[768,2304]{1,0:T(8,128)(2,1)} %enc_qkv.1, bf16[768,768]{1,0:T(8,128)(2,1)} %enc_wo.1, ...), custom_call_target="tpu_custom_call" | custom-call | tf_op jit(solution)/shard_map/step_of_one_example/pallas_call | solution.py:859
  125.4 3.0 %lamb.1 = (f32[1]{0:T(128)}, f32[1]{0:T(128)}, f32[2]{0:T(128)}, f32[100,768]{1,0:T(8,128)}, f32[100,768]{1,0:T(8,128)}, /*index=5*/f32[100,768]{1,0:T(8,128)}) custom-call(f32[4,32,768]{2,1,0:T(8,128)} %step_of_one_example.1.summed, f32[100,768]{1,0:T(8,128)} %first_old.1, f32[100,768]{1,0:T(8,128)} %second_old.1, f32[100,768]{1,0:T(8,128)} %prompt.3), custom_call_target="tpu_custom_call" | custom-call | tf_op jit(solution)/shard_map/lamb/pallas_call | solution.py:1055
Async XLA Ops:
  12.1 0.7 copy-start.1
  12.8 13.0 %copy-start.2 = (bf16[768,2,384]{2,1,0:T(2,128)(2,1)S(1)}, bf16[768,2,384]{2,1,0:T(2,128)(2,1)}, u32[]{:S(2)}) copy-start(bf16[768,2,384]{2,1,0:T(2,128)(2,1)} %param.38) | copy-start | bytes 3538948
  24.8 1.0 copy-start

commit v2 on v1

--- a/solution.py
+++ b/solution.py
@@ -95,7 +95,7 @@
     return pl.ds(pl.multiple_of(base + index * size, LANES), size)
 
 
-UNROLL = {"attend": 1, "self": 1, "cross": 3, "cross_back": 3, "lead": 1, "vocab": 2}
+UNROLL = {"attend": 2, "self": 1, "cross": 3, "cross_back": 3, "lead": 1, "vocab": 2}
 
 
 def main_kernel(

time: 129 us -> 128 us (level)
  no operation moved by 1% of the time
where the time goes in v2:
time: 128 us
  Pallas kernels  124 us (97%)
  local copies, waits for them, and re-layouts  2.95 us (2%)
    pallas_call x1, Pallas kernels, main_call(): pl.pallas_call(main_kernel, out_shape=jax.ShapeDtypeStruct((QUARTERS, LEA...  97.9 us
    pallas_call x1, Pallas kernels, lookup_call(): pl.pallas_call(functools.partial(lookup_kernel, rows, tokens, lead, enc_d...  12 us
    pallas_call x1, Pallas kernels, ids_call(): pl.pallas_call(ids_kernel, out_shape=jax.ShapeDtypeStruct((seqs, lanes),...  11.5 us
    pallas_call x1, Pallas kernels, lamb_call(): pl.pallas_call(lamb_kernel, out_shape=(jax.ShapeDtypeStruct((1,), F32), j...  2.98 us
    unnamed x7, local copies, waits for them, and re-layouts  2.95 us

profile of v2, /device:TPU:1, one launch (start us, length us, event | category | flops | bytes accessed | tf_op | source)
XLA Modules:
  0.0 128.2 jit_solution(13391809920528973960)
XLA Ops:
  0.6 11.5 %ids_of_one_example.1.ids = s32[16,128]{1,0:T(8,128)} custom-call(s32[8,64]{1,0:T(8,128)} %enc_ids.1, s32[8,8]{1,0:T(8,128)} %dec_ids.1, s32[8,8]{1,0:T(8,128)} %target_ids.1), custom_call_target="tpu_custom_call" | custom-call | tf_op jit(solution)/shard_map/ids_of_one_example/pallas_call | solution.py:919
  12.1 0.0 copy-start.1
  12.1 0.7 copy-done.1
  12.8 0.0 copy-start.2
  12.8 12.0 %embedding_rows.1.picked = bf16[704,768]{1,0:T(8,128)(2,1)S(1)} custom-call(s32[16,128]{1,0:T(8,128)S(1)} %copy-done.1, bf16[16064,768]{1,0:T(8,128)(2,1)} %embedding.1), custom_call_target="tpu_custom_call" | custom-call | tf_op jit(solution)/shard_map/embedding_rows/pallas_call | solution.py:1010
  24.8 0.0 copy-start
  24.8 1.0 copy-done
  25.8 0.0 copy-done.2
  25.8 1.3 copy.27
  27.1 97.9 %step_of_one_example.1.summed = f32[4,32,768]{2,1,0:T(8,128)} custom-call(s32[8]{0:T(128)} %lengths.1, bf16[704,768]{1,0:T(8,128)(2,1)} %copy-done, f32[100,768]{1,0:T(8,128)} %prompt.3, s32[8,128]{1,0:T(8,128)} %loss_mask.1, f32[7,768]{1,0:T(8,128)} %gains.1, bf16[768,2304]{1,0:T(8,128)(2,1)} %enc_qkv.1, bf16[768,768]{1,0:T(8,128)(2,1)} %enc_wo.1, ...), custom_call_target="tpu_custom_call" | custom-call | tf_op jit(solution)/shard_map/step_of_one_example/pallas_call | solution.py:859
  125.0 3.0 %lamb.1 = (f32[1]{0:T(128)}, f32[1]{0:T(128)}, f32[2]{0:T(128)}, f32[100,768]{1,0:T(8,128)}, f32[100,768]{1,0:T(8,128)}, /*index=5*/f32[100,768]{1,0:T(8,128)}) custom-call(f32[4,32,768]{2,1,0:T(8,128)} %step_of_one_example.1.summed, f32[100,768]{1,0:T(8,128)} %first_old.1, f32[100,768]{1,0:T(8,128)} %second_old.1, f32[100,768]{1,0:T(8,128)} %prompt.3), custom_call_target="tpu_custom_call" | custom-call | tf_op jit(solution)/shard_map/lamb/pallas_call | solution.py:1055
Async XLA Ops:
  12.1 0.7 copy-start.1
  12.8 13.0 %copy-start.2 = (bf16[768,2,384]{2,1,0:T(2,128)(2,1)S(1)}, bf16[768,2,384]{2,1,0:T(2,128)(2,1)}, u32[]{:S(2)}) copy-start(bf16[768,2,384]{2,1,0:T(2,128)(2,1)} %param.38) | copy-start | bytes 3538948
  24.8 1.0 copy-start
